TPU v7x, 32 devices: a whole 2x2x4 slice. The times are simulated.
32 devices in a mesh: dp: 8 (over y, x, core), tensor: 4 (over z).
Axes of the slice: x: 2, y: 2, z: 4, core: 2. Of those that a mesh axis runs over, the one named last changes fastest.
Arguments:
- inputs: bfloat16 [1024, 8192], P('dp', 'tensor'), may hold values from -6 to 6
- cotangent: bfloat16 [1024, 8192], P('dp', 'tensor'), may hold values from -6 to 6
- w_first: bfloat16 [32, 256, 256], P('tensor'), may hold values from -0.375 to 0.375
- w_second: bfloat16 [32, 256, 896], P('tensor'), may hold values from -0.375 to 0.375
- w_third: bfloat16 [32, 896, 256], P('tensor'), may hold values from -0.1875 to 0.1875
- w_fourth: bfloat16 [32, 256, 256], P('tensor'), may hold values from -0.375 to 0.375
- route_up: int32 [8192], replicated, may hold values from 0 to 8191, as said below
- route_down: int32 [8192], replicated, may hold values from 0 to 8191, as said below
Outputs:
- layer_out: bfloat16 [1024, 8192], P('dp', 'tensor')
- grad_input: bfloat16 [1024, 8192], P('dp', 'tensor')
- grad_first: float32 [32, 256, 256], P('tensor', 'dp')
- grad_second: float32 [32, 256, 896], P('tensor', 'dp')
- grad_third: float32 [32, 896, 256], P('tensor', 'dp')
- grad_fourth: float32 [32, 256, 256], P('tensor', 'dp')
Inputs may be any that keep to these rules, and one draw needn't show every extreme that they name: `route_up`: A permutation of 0 .. 8191. For every destination block b (positions b * 256 to (b + 1) * 256 - 1), its sources contain exactly 8 features of each of the 32 source blocks. `route_down`: same law as route_up, drawn independently.
All inputs are finite; a program needn't handle non-finite values.
Results may differ from a plain program's by a relative error of at most 0.011.
Values may be sent and summed in bfloat16 or wider, within the bound.
A program may use at most 128 MiB of HBM per device.

v0:
```python
import functools
import math

import jax
import jax.numpy as jnp
from jax import lax
from jax.experimental import pallas as pl
from jax.experimental.pallas import tpu as pltpu
from jax.sharding import PartitionSpec as P


def blocks(z, w):
    rows = z.shape[0]
    nblk, fin, fout = w.shape
    out = jnp.einsum(
        "tli,lio->tlo", z.reshape(rows, nblk, fin), w, preferred_element_type=jnp.float32
    )
    return out.reshape(rows, nblk * fout)


def blocks_back(g, w):
    rows = g.shape[0]
    nblk, fin, fout = w.shape
    out = jnp.einsum(
        "tlo,lio->tli", g.reshape(rows, nblk, fout), w, preferred_element_type=jnp.float32
    )
    return out.reshape(rows, nblk * fin)


def block_grad(z, g, nblk, scale):
    rows = z.shape[0]
    total = jnp.einsum(
        "tli,tlo->lio",
        z.reshape(rows, nblk, -1),
        g.reshape(rows, nblk, -1),
        preferred_element_type=jnp.float32,
    )
    return total * scale


def gelu_tanh(v):
    return jax.nn.gelu(v, approximate=True)


def route_tables(route_all, width, ranks, rank):
    pieces = width // ranks
    grid = route_all.reshape(ranks, width)
    owner = grid // width
    local_col = grid - owner * width
    owner_hot = owner[:, :, None] == jnp.arange(ranks, dtype=jnp.int32)[None, None, :]
    counted = jnp.cumsum(owner_hot.astype(jnp.int32), axis=1)
    position = jnp.sum(jnp.where(owner_hot, counted, 0), axis=2) - 1
    recv_slot = owner * pieces + position
    my_slots = lax.dynamic_index_in_dim(recv_slot, rank, axis=0, keepdims=False)
    lanes = jnp.arange(width, dtype=jnp.int32)
    place_mat = (lanes[:, None] == my_slots[None, :]).astype(jnp.bfloat16)
    send_slot = (jnp.arange(ranks, dtype=jnp.int32)[:, None] * pieces + position).reshape(-1)
    owned = (owner == rank).reshape(-1)
    flat_col = local_col.reshape(-1)
    picks = jnp.logical_and(owned[None, :], send_slot[None, :] == lanes[:, None])
    col_of_slot = jnp.sum(jnp.where(picks, flat_col[None, :], 0), axis=1)
    send_mat = (lanes[:, None] == col_of_slot[None, :]).astype(jnp.bfloat16)
    return (send_mat, place_mat)


def apply_perm(x, table):
    return jnp.dot(x, table, preferred_element_type=jnp.float32).astype(jnp.bfloat16)


def apply_back(x, table):
    return lax.dot_general(
        x, table, (((1,), (1,)), ((), ())), preferred_element_type=jnp.float32
    ).astype(jnp.bfloat16)


def body(inputs, cotangent, w_first, w_second, w_third, w_fourth, route_up, route_down):
    ranks = lax.axis_size("tensor")
    rank = lax.axis_index("tensor")
    tok = inputs.shape[0]
    width = inputs.shape[1]
    pieces = width // ranks
    nblk = w_first.shape[0]
    scale = 1.0 / math.sqrt(tok * lax.axis_size("dp"))
    up_send, up_place = route_tables(route_up, width, ranks, rank)
    down_send, down_place = route_tables(route_down, width, ranks, rank)
    first_act = blocks(inputs, w_first).astype(jnp.bfloat16)
    outgoing = apply_perm(first_act, up_send).reshape(tok, ranks, pieces)
    received = lax.all_to_all(outgoing, "tensor", split_axis=1, concat_axis=1, tiled=True)
    mixed = apply_perm(received.reshape(received.shape[0], width), up_place)
    mixed_up = mixed
    pre_act = blocks(mixed, w_second).astype(jnp.bfloat16)
    pre_float = pre_act.astype(jnp.float32)
    hidden_act = gelu_tanh(pre_float).astype(jnp.bfloat16)
    third_act = blocks(hidden_act, w_third).astype(jnp.bfloat16)
    outgoing = apply_perm(third_act, down_send).reshape(tok, ranks, pieces)
    received = lax.all_to_all(outgoing, "tensor", split_axis=1, concat_axis=1, tiled=True)
    mixed = apply_perm(received.reshape(received.shape[0], width), down_place)
    layer_out = blocks(mixed, w_fourth).astype(jnp.bfloat16)
    back_mixed_down = blocks_back(cotangent, w_fourth).astype(jnp.bfloat16)
    grad_fourth = block_grad(mixed, cotangent, nblk, scale)
    returning = apply_back(back_mixed_down, down_place).reshape(tok, ranks, pieces)
    received = lax.all_to_all(returning, "tensor", split_axis=1, concat_axis=1, tiled=True)
    back = apply_back(received.reshape(received.shape[0], width), down_send)
    back_third = back
    back_hidden = blocks_back(back, w_third)
    grad_third = block_grad(hidden_act, back_third, nblk, scale)
    pull = jax.vjp(gelu_tanh, pre_float)[1]
    back_pre = pull(back_hidden)[0].astype(jnp.bfloat16)
    grad_second = block_grad(mixed_up, back_pre, nblk, scale)
    back_mixed_up = blocks_back(back_pre, w_second).astype(jnp.bfloat16)
    returning = apply_back(back_mixed_up, up_place).reshape(tok, ranks, pieces)
    received = lax.all_to_all(returning, "tensor", split_axis=1, concat_axis=1, tiled=True)
    back = apply_back(received.reshape(received.shape[0], width), up_send)
    grad_input = blocks_back(back, w_first).astype(jnp.bfloat16)
    grad_first = block_grad(inputs, back, nblk, scale)
    def shared(total):
        return lax.psum_scatter(
            total.astype(jnp.bfloat16), "dp", scatter_dimension=1, tiled=True
        ).astype(jnp.float32)

    return (
        layer_out, grad_input, shared(grad_first), shared(grad_second),
        shared(grad_third), shared(grad_fourth),
    )


MESH = pl.DeviceIdType.MESH
NN = (((1,), (0,)), ((), ()))
NT = (((1,), (1,)), ((), ()))
TN = (((0,), (0,)), ((), ()))
GELU_C = 0.7978845608
GELU_A = 0.044715


def mm(a, b, dims):
    return lax.dot_general(a, b, dims, preferred_element_type=jnp.float32)


def route_slots(routes, nb, ranks, rank):
    bw = routes.shape[-1]
    share = bw // nb
    nblk = nb // ranks
    src = routes // bw
    col = routes - src * bw
    hot = src[:, :, None, :] == jnp.arange(nb, dtype=jnp.int32)[None, None, :, None]
    upto = jnp.arange(bw)[:, None] <= jnp.arange(bw)[None, :]
    counted = jnp.einsum(
        "zbsk,kl->zbsl",
        hot.astype(jnp.bfloat16),
        upto.astype(jnp.bfloat16),
        preferred_element_type=jnp.float32,
    )
    j = jnp.sum(jnp.where(hot, counted, 0.0), axis=2).astype(jnp.int32) - 1
    slot = src * share + j
    mine = lax.dynamic_slice_in_dim(slot, rank * nblk, nblk, 1)
    local = slot - rank * (nblk * share)
    m = jnp.arange(nblk * share, dtype=jnp.int32)[None, None, :, None]
    cols = jnp.sum(jnp.where(local[:, :, None, :] == m, col[:, :, None, :], 0), axis=3)
    cols = cols.reshape(2, nb, nblk, share).transpose(0, 1, 3, 2).reshape(2, bw, nblk)
    return mine, cols


def layer_kernel(ranks, nblk, tok, bw, hw, scale, inp, cot, w1, w2, w3, w4, slot, cols,
                 out, gin, o1, o2, o3, o4,
                 pmat, smat, act, mup, mdn, bth, bfs, pre, hid, bpr, stage, sbuf, rbuf,
                 g1, g2, g3, g4, a1, a2, a3, a4, b1, b2, b3, b4, c1, c2, c3, c4,
                 ssem, rsem, asend, arecv, bsend, brecv, csend, crecv):
    bf = jnp.bfloat16
    rank = lax.axis_index("tensor")
    dp = lax.axis_index("dp")
    core = dp % 2
    x = (dp // 2) % 2
    y = dp // 4
    to_core = dp + 1 - 2 * core
    to_x = dp + 2 - 4 * x
    to_y = dp + 4 - 8 * y
    share = bw // (nblk * ranks)
    part = nblk * share
    half = nblk // 2
    gs, ras, rbs, rcs, outs = (g1, g2, g3, g4), (a1, a2, a3, a4), (b1, b2, b3, b4), (c1, c2, c3, c4), (o1, o2, o3, o4)

    barrier = pltpu.get_barrier_semaphore()
    for k in range(1, ranks):
        pl.semaphore_signal(barrier, inc=1, device_id=(dp, (rank + k) % ranks), device_id_type=MESH)
    for peer in (to_core, to_x, to_y):
        pl.semaphore_signal(barrier, inc=1, device_id=(peer, rank), device_id_type=MESH)

    lane = lax.broadcasted_iota(jnp.int32, (bw, bw), 1)
    row = lax.broadcasted_iota(jnp.int32, (bw, bw), 0)

    def make_smat(z):
        for s in range(nblk):
            smat[z, s] = (cols[z, :, s:s + 1] == lane).astype(jnp.float32).astype(bf)

    def make_pmat(z):
        for d in range(nblk):
            pmat[z, d] = (slot[z, d:d + 1, :] == row).astype(jnp.float32).astype(bf)

    def blk(b):
        return pl.ds(pl.multiple_of(b * bw, bw), bw)

    def each(step):
        def one(b, carry):
            step(b)
            return carry
        lax.fori_loop(0, nblk, one, 0)

    def hop(e, k):
        peer = (rank + k) % ranks
        return pltpu.make_async_remote_copy(
            src_ref=sbuf.at[e, peer], dst_ref=rbuf.at[e, rank],
            send_sem=ssem.at[e, k - 1], recv_sem=rsem.at[e, k - 1],
            device_id=(dp, peer), device_id_type=MESH)

    def send(e):
        for k in (2, 1, 3) if ranks == 4 else range(1, ranks):
            hop(e, k).start()
        rbuf[e, rank] = sbuf[e, rank]

    def arrive(e):
        for k in range(1, ranks):
            hop(e, k).wait_recv()

    def sort_out(z, b, value):
        rows = mm(smat[z, b], value, NT).reshape(ranks, nblk, share, tok)
        stage[:, :, pl.ds(pl.multiple_of(b * share, share), share), :] = rows

    def send_sorted(e):
        sbuf[e] = stage[...].astype(bf)
        send(e)

    def placed(e, z, b):
        return mm(rbuf[e, :, b].reshape(bw, tok), pmat[z, b], TN).astype(bf)

    def unplace(e, z, b, value):
        sbuf[e, :, b] = mm(pmat[z, b], value, NT).astype(bf).reshape(ranks, part, tok)

    def unsorted(z, b):
        rows = stage[:, :, pl.ds(pl.multiple_of(b * share, share), share), :]
        return mm(rows.reshape(bw, tok).astype(bf), smat[z, b], TN).astype(bf)

    def put_grad(w, b, left, right):
        term = (mm(left, right, TN) * scale).astype(bf)
        gs[w][:, :, :, b] = term.reshape((2, 2, 2) + gs[w].shape[4:])

    def copy_a(w):
        return pltpu.make_async_remote_copy(
            src_ref=gs[w].at[:, :, 1 - core], dst_ref=ras[w],
            send_sem=asend.at[w], recv_sem=arecv.at[w],
            device_id=(to_core, rank), device_id_type=MESH)

    lo, hi = pl.ds(0, half), pl.ds(half, half)

    def copies_b(w):
        return (
            pltpu.make_async_remote_copy(
                src_ref=ras[w].at[:, 1 - x, lo], dst_ref=rbs[w].at[:, lo],
                send_sem=bsend.at[w, 0], recv_sem=brecv.at[w, 0],
                device_id=(to_x, rank), device_id_type=MESH),
            pltpu.make_async_remote_copy(
                src_ref=ras[w].at[1 - y, :, hi], dst_ref=rbs[w].at[:, hi],
                send_sem=bsend.at[w, 1], recv_sem=brecv.at[w, 1],
                device_id=(to_y, rank), device_id_type=MESH))

    def copies_c(w):
        return (
            pltpu.make_async_remote_copy(
                src_ref=rbs[w].at[1 - y, lo], dst_ref=rcs[w].at[lo],
                send_sem=csend.at[w, 0], recv_sem=crecv.at[w, 0],
                device_id=(to_y, rank), device_id_type=MESH),
            pltpu.make_async_remote_copy(
                src_ref=rbs[w].at[1 - x, hi], dst_ref=rcs[w].at[hi],
                send_sem=csend.at[w, 1], recv_sem=crecv.at[w, 1],
                device_id=(to_x, rank), device_id_type=MESH))

    def f32(v):
        return v.astype(jnp.float32)

    def a_to_b(w):
        copy_a(w).wait_recv()

        def step(b):
            ras[w][:, :, b] = (f32(ras[w][:, :, b]) + f32(gs[w][:, :, core, b])).astype(bf)
        each(step)
        for c in copies_b(w):
            c.start()

    def b_to_c(w):
        for c in copies_b(w):
            c.wait_recv()

        def one(b, carry):
            rbs[w][:, b] = (f32(rbs[w][:, b]) + f32(ras[w][:, x, b])).astype(bf)
            rbs[w][:, b + half] = (f32(rbs[w][:, b + half]) + f32(ras[w][y, :, b + half])).astype(bf)
            return carry
        lax.fori_loop(0, half, one, 0)
        for c in copies_c(w):
            c.start()

    def finish(w):
        for c in copies_c(w):
            c.wait_recv()

        def one(b, carry):
            outs[w][b] = f32(rbs[w][y, b]) + f32(rcs[w][b])
            outs[w][b + half] = f32(rbs[w][x, b + half]) + f32(rcs[w][b + half])
            return carry
        lax.fori_loop(0, half, one, 0)

    make_smat(0)

    def first(b):
        sort_out(0, b, mm(inp[:, blk(b)], w1[b], NN).astype(bf))
    each(first)
    pl.semaphore_wait(barrier, ranks - 1 + 3)
    send_sorted(0)

    make_pmat(1)

    def back_fourth(b):
        unplace(1, 1, b, mm(cot[:, blk(b)], w4[b], NT).astype(bf))
    each(back_fourth)
    send(1)
    make_pmat(0)
    make_smat(1)

    arrive(0)

    def middle(b):
        m = placed(0, 0, b)
        mup[b] = m
        p = mm(m, w2[b], NN).astype(bf)
        pre[b] = p
        v = f32(p)
        h = (0.5 * v * (1.0 + jnp.tanh(GELU_C * (v + GELU_A * (v * v * v))))).astype(bf)
        hid[b] = h
        sort_out(1, b, mm(h, w3[b], NN).astype(bf))
    each(middle)
    send_sorted(2)

    arrive(1)
    stage[...] = f32(rbuf[1])

    def third(b):
        t = unsorted(1, b)
        bth[b] = t
        put_grad(2, b, hid[b], t)
    each(third)
    copy_a(2).start()

    def back_second(b):
        v = f32(pre[b])
        v2 = v * v
        th = jnp.tanh(GELU_C * (v + GELU_A * (v2 * v)))
        slope = 0.5 * (1.0 + th) + 0.5 * v * (1.0 - th * th) * (GELU_C * (1.0 + 3.0 * GELU_A * v2))
        p = (mm(bth[b], w3[b], NT) * slope).astype(bf)
        bpr[b] = p
        unplace(3, 0, b, mm(p, w2[b], NT).astype(bf))
    each(back_second)
    send(3)

    a_to_b(2)

    def second(b):
        put_grad(1, b, mup[b], bpr[b])
    each(second)
    copy_a(1).start()

    arrive(2)

    def fourth(b):
        m = placed(2, 1, b)
        out[:, blk(b)] = mm(m, w4[b], NN).astype(bf)
        put_grad(3, b, m, cot[:, blk(b)])
    each(fourth)
    copy_a(3).start()
    a_to_b(1)
    a_to_b(3)

    arrive(3)
    stage[...] = f32(rbuf[3])

    def last(b):
        t = unsorted(0, b)
        put_grad(0, b, inp[:, blk(b)], t)
        gin[:, blk(b)] = mm(t, w1[b], NT).astype(bf)
    each(last)
    copy_a(0).start()
    a_to_b(0)
    for w in (2, 1, 3, 0):
        b_to_c(w)
    for w in (2, 1, 3, 0):
        finish(w)

    for e in range(4):
        for k in range(1, ranks):
            hop(e, k).wait_send()
    for w in range(4):
        copy_a(w).wait_send()
        for c in copies_b(w) + copies_c(w):
            c.wait_send()


def fused_body(inputs, cotangent, w_first, w_second, w_third, w_fourth, route_up, route_down):
    ranks = lax.axis_size("tensor")
    dps = lax.axis_size("dp")
    rank = lax.axis_index("tensor")
    tok, width = inputs.shape
    nblk, bw, hw = w_second.shape
    nb = nblk * ranks
    part = bw // ranks
    scale = 1.0 / math.sqrt(tok * dps)
    routes = jnp.stack([route_up, route_down]).reshape(2, nb, bw)
    slot, cols = route_slots(routes, nb, ranks, rank)
    weights = (w_first, w_second, w_third, w_fourth)
    shapes = [(w.shape[1] // dps, w.shape[2]) for w in weights]
    bf = jnp.bfloat16
    vm = pltpu.VMEM
    scratch = [
        vm((2, nblk, bw, bw), bf), vm((2, nblk, bw, bw), bf),
        vm((nblk, tok, bw), bf), vm((nblk, tok, bw), bf), vm((nblk, tok, bw), bf),
        vm((nblk, tok, bw), bf), vm((nblk, tok, bw), bf),
        vm((nblk, tok, hw), bf), vm((nblk, tok, hw), bf), vm((nblk, tok, hw), bf),
        vm((ranks, nblk, part, tok), jnp.float32),
        vm((4, ranks, nblk, part, tok), bf), vm((4, ranks, nblk, part, tok), bf),
    ]
    scratch += [vm((2, 2, 2, nblk) + s, bf) for s in shapes]
    scratch += [vm((2, 2, nblk) + s, bf) for s in shapes]
    scratch += [vm((2, nblk) + s, bf) for s in shapes]
    scratch += [vm((nblk,) + s, bf) for s in shapes]
    dma = pltpu.SemaphoreType.DMA
    scratch += [dma((4, ranks - 1)), dma((4, ranks - 1)), dma((4,)), dma((4,))]
    scratch += [dma((4, 2))] * 4
    out_shape = [jax.ShapeDtypeStruct((tok, width), bf)] * 2
    out_shape += [jax.ShapeDtypeStruct((nblk,) + s, jnp.float32) for s in shapes]
    spec = pl.BlockSpec(memory_space=pltpu.VMEM)
    return tuple(pl.pallas_call(
        functools.partial(layer_kernel, ranks, nblk, tok, bw, hw, scale),
        out_shape=out_shape,
        in_specs=[spec] * 8,
        out_specs=[spec] * 6,
        scratch_shapes=scratch,
        compiler_params=pltpu.CompilerParams(
            collective_id=0, has_side_effects=True, vmem_limit_bytes=60 * 1024 * 1024),
    )(inputs, cotangent, *weights, slot, cols))


def solution(mesh):
    def pick(*args):
        inputs, w_first, w_third = args[0], args[2], args[4]
        ranks, dps = mesh.shape["tensor"], mesh.shape["dp"]
        nblk, bw = w_first.shape[:2]
        aligned = (
            dps == 8 and nblk % 2 == 0 and bw // (nblk * ranks) == 8
            and (bw // dps) % 16 == 0 and (w_third.shape[1] // dps) % 16 == 0
            and (bw // ranks) % 16 == 0 and inputs.shape[0] % 128 == 0
        )
        return (fused_body if aligned else body)(*args)

    return jax.shard_map(
        pick,
        mesh=mesh,
        in_specs=(
            P("dp", "tensor"),
            P("dp", "tensor"),
            P("tensor", None, None),
            P("tensor", None, None),
            P("tensor", None, None),
            P("tensor", None, None),
            P(),
            P(),
        ),
        out_specs=(
            P("dp", "tensor"),
            P("dp", "tensor"),
            P("tensor", "dp", None),
            P("tensor", "dp", None),
            P("tensor", "dp", None),
            P("tensor", "dp", None),
        ),
        check_vma=False,
    )
```

profile of v0, /device:TPU:8, one launch (start us, length us, event | category | flops | bytes accessed | tf_op | source)
XLA Modules:
  0.0 105.6 jit_solution(17683483955928374039)
XLA Ops:
  0.6 0.8 stack.9
  1.4 0.8 stack.10
  2.3 0.7 select_reduce_fusion.1
  3.0 0.1 broadcast_subtract_fusion
  3.0 1.2 %select_reduce_fusion = s32[2,32,64]{2,1,0:T(8,128)S(1)} fusion(s32[2,32,256]{2,1,0:T(8,128)S(1)} %get-tuple-element.8, s32[2,32,256]{2,1,0:T(8,128)S(1)} %get-tuple-element.6), kind=kLoop, calls=%fused_computation | loop fusion | flops 3141632 | bytes 147456 | tf_op jit(solution)/shard_map/reduce_sum | solution.py:158
  4.2 0.6 constant_dynamic-slice_fusion.slot
  4.8 0.1 copy.15
  4.9 0.8 copy.16
  5.8 90.5 %shard_map.127 = (bf16[128,2048]{1,0:T(8,128)(2,1)}, bf16[128,2048]{1,0:T(8,128)(2,1)}, f32[8,32,256]{2,1,0:T(8,128)}, f32[8,32,896]{2,1,0:T(8,128)}, f32[8,112,256]{2,1,0:T(8,128)}, /*index=5*/f32[8,32,256]{2,1,0:T(8,128)}) custom-call(bf16[128,2048]{1,0:T(8,128)(2,1)} %inp.1, bf16[128,2048]{1,0:T(8,128)(2,1)} %cot.1, bf16[8,256,256]{2,1,0:T(8,128)(2,1)} %w1.1, ...), custom_call_target="tpu_custom_call" | custom-call | tf_op jit(solution)/shard_map/pallas_call | solution.py:437
  96.2 0.0 copy-start
  96.2 0.0 copy-start.1
  96.2 2.0 %copy.25 = bf16[128,2048]{1,0:T(8,128)(2,1)} copy(bf16[128,2048]{1,0:T(8,128)(2,1)} %get-tuple-element.15) | data formatting | bytes 1048576
  98.2 1.9 %copy.26 = bf16[128,2048]{1,0:T(8,128)(2,1)} copy(bf16[128,2048]{1,0:T(8,128)(2,1)} %get-tuple-element.16) | data formatting | bytes 1048576
  100.1 1.7 %copy.27 = f32[8,32,256]{2,1,0:T(8,128)} copy(f32[8,32,256]{2,1,0:T(8,128)} %get-tuple-element.17) | data formatting | bytes 524288
  101.8 2.2 %copy.28 = f32[8,32,896]{2,1,0:T(8,128)} copy(f32[8,32,896]{2,1,0:T(8,128)} %get-tuple-element.18) | data formatting | bytes 1835008
  103.9 0.0 copy-done
  103.9 0.9 copy.29
  104.9 0.0 copy-done.1
  104.9 0.7 copy.30
  (3 shorter events, 0.1 us)
Async XLA Ops:
  96.2 7.7 %copy-start = (f32[8,112,256]{2,1,0:T(8,128)S(1)}, f32[8,112,256]{2,1,0:T(8,128)}, u32[]{:S(2)}) copy-start(f32[8,112,256]{2,1,0:T(8,128)} %get-tuple-element.19) | copy-start | bytes 2752516
  96.2 8.6 %copy-start.1 = (f32[8,32,256]{2,1,0:T(8,128)S(1)}, f32[8,32,256]{2,1,0:T(8,128)}, u32[]{:S(2)}) copy-start(f32[8,32,256]{2,1,0:T(8,128)} %get-tuple-element.20) | copy-start | bytes 786436
where the time goes:
time: 106 us
  Pallas kernels  90.5 us (85%)
  local copies, waits for them, and re-layouts  12.4 us (12%)
  other arithmetic  1.26 us (1%)
    pallas_call x1, Pallas kernels, fused_body(): pl.pallas_call(functools.partial(layer_kernel, ranks, nblk, tok, bw, hw,...  90.5 us
    unnamed x11, local copies, waits for them, and re-layouts  9.33 us

commit v1 on v0

--- a/solution.py
+++ b/solution.py
@@ -176,7 +176,8 @@
     to_y = dp + 4 - 8 * y
     share = bw // (nblk * ranks)
     part = nblk * share
-    half = nblk // 2
+    hb = nblk // 2
+    quarter = hb // 2
     gs, ras, rbs, rcs, outs = (g1, g2, g3, g4), (a1, a2, a3, a4), (b1, b2, b3, b4), (c1, c2, c3, c4), (o1, o2, o3, o4)
 
     barrier = pltpu.get_barrier_semaphore()
@@ -199,36 +200,39 @@
     def blk(b):
         return pl.ds(pl.multiple_of(b * bw, bw), bw)
 
-    def each(step):
+    def each(step, c=None):
         def one(b, carry):
             step(b)
             return carry
-        lax.fori_loop(0, nblk, one, 0)
-
-    def hop(e, k):
+        lax.fori_loop(*((0, nblk) if c is None else (c * hb, c * hb + hb)), one, 0)
+
+    def piece(e, c):
+        if e in (0, 3):
+            return pl.ds(c * hb, hb), slice(None)
+        return slice(None), pl.ds(c * hb * share, hb * share)
+
+    def hop(e, c, k):
         peer = (rank + k) % ranks
+        rows, cut = piece(e, c)
         return pltpu.make_async_remote_copy(
-            src_ref=sbuf.at[e, peer], dst_ref=rbuf.at[e, rank],
-            send_sem=ssem.at[e, k - 1], recv_sem=rsem.at[e, k - 1],
+            src_ref=sbuf.at[e, peer, rows, cut], dst_ref=rbuf.at[e, rank, rows, cut],
+            send_sem=ssem.at[e, c, k - 1], recv_sem=rsem.at[e, c, k - 1],
             device_id=(dp, peer), device_id_type=MESH)
 
-    def send(e):
+    def send(e, c):
         for k in (2, 1, 3) if ranks == 4 else range(1, ranks):
-            hop(e, k).start()
-        rbuf[e, rank] = sbuf[e, rank]
-
-    def arrive(e):
+            hop(e, c, k).start()
+        rows, cut = piece(e, c)
+        rbuf[e, rank, rows, cut] = sbuf[e, rank, rows, cut]
+
+    def arrive(e, c):
         for k in range(1, ranks):
-            hop(e, k).wait_recv()
+            hop(e, c, k).wait_recv()
 
     def sort_out(z, b, value):
         rows = mm(smat[z, b], value, NT).reshape(ranks, nblk, share, tok)
         stage[:, :, pl.ds(pl.multiple_of(b * share, share), share), :] = rows
 
-    def send_sorted(e):
-        sbuf[e] = stage[...].astype(bf)
-        send(e)
-
     def placed(e, z, b):
         return mm(rbuf[e, :, b].reshape(bw, tok), pmat[z, b], TN).astype(bf)
 
@@ -243,69 +247,75 @@
         term = (mm(left, right, TN) * scale).astype(bf)
         gs[w][:, :, :, b] = term.reshape((2, 2, 2) + gs[w].shape[4:])
 
-    def copy_a(w):
+    def copy_a(w, c):
         return pltpu.make_async_remote_copy(
-            src_ref=gs[w].at[:, :, 1 - core], dst_ref=ras[w],
-            send_sem=asend.at[w], recv_sem=arecv.at[w],
+            src_ref=gs[w].at[:, :, 1 - core, pl.ds(c * hb, hb)],
+            dst_ref=ras[w].at[:, :, pl.ds(c * hb, hb)],
+            send_sem=asend.at[w, c], recv_sem=arecv.at[w, c],
             device_id=(to_core, rank), device_id_type=MESH)
 
-    lo, hi = pl.ds(0, half), pl.ds(half, half)
-
-    def copies_b(w):
+    def spans(c):
+        return pl.ds(c * hb, quarter), pl.ds(c * hb + quarter, quarter)
+
+    def copies_b(w, c):
+        lo, hi = spans(c)
         return (
             pltpu.make_async_remote_copy(
                 src_ref=ras[w].at[:, 1 - x, lo], dst_ref=rbs[w].at[:, lo],
-                send_sem=bsend.at[w, 0], recv_sem=brecv.at[w, 0],
+                send_sem=bsend.at[w, c, 0], recv_sem=brecv.at[w, c, 0],
                 device_id=(to_x, rank), device_id_type=MESH),
             pltpu.make_async_remote_copy(
                 src_ref=ras[w].at[1 - y, :, hi], dst_ref=rbs[w].at[:, hi],
-                send_sem=bsend.at[w, 1], recv_sem=brecv.at[w, 1],
+                send_sem=bsend.at[w, c, 1], recv_sem=brecv.at[w, c, 1],
                 device_id=(to_y, rank), device_id_type=MESH))
 
-    def copies_c(w):
+    def copies_c(w, c):
+        lo, hi = spans(c)
         return (
             pltpu.make_async_remote_copy(
                 src_ref=rbs[w].at[1 - y, lo], dst_ref=rcs[w].at[lo],
-                send_sem=csend.at[w, 0], recv_sem=crecv.at[w, 0],
+                send_sem=csend.at[w, c, 0], recv_sem=crecv.at[w, c, 0],
                 device_id=(to_y, rank), device_id_type=MESH),
             pltpu.make_async_remote_copy(
                 src_ref=rbs[w].at[1 - x, hi], dst_ref=rcs[w].at[hi],
-                send_sem=csend.at[w, 1], recv_sem=crecv.at[w, 1],
+                send_sem=csend.at[w, c, 1], recv_sem=crecv.at[w, c, 1],
                 device_id=(to_x, rank), device_id_type=MESH))
 
     def f32(v):
         return v.astype(jnp.float32)
 
-    def a_to_b(w):
-        copy_a(w).wait_recv()
+    def a_to_b(w, c):
+        copy_a(w, c).wait_recv()
 
         def step(b):
             ras[w][:, :, b] = (f32(ras[w][:, :, b]) + f32(gs[w][:, :, core, b])).astype(bf)
-        each(step)
-        for c in copies_b(w):
-            c.start()
-
-    def b_to_c(w):
-        for c in copies_b(w):
-            c.wait_recv()
+        each(step, c)
+        for copy in copies_b(w, c):
+            copy.start()
+
+    def b_to_c(w, c):
+        for copy in copies_b(w, c):
+            copy.wait_recv()
 
         def one(b, carry):
             rbs[w][:, b] = (f32(rbs[w][:, b]) + f32(ras[w][:, x, b])).astype(bf)
-            rbs[w][:, b + half] = (f32(rbs[w][:, b + half]) + f32(ras[w][y, :, b + half])).astype(bf)
+            h = b + quarter
+            rbs[w][:, h] = (f32(rbs[w][:, h]) + f32(ras[w][y, :, h])).astype(bf)
             return carry
-        lax.fori_loop(0, half, one, 0)
-        for c in copies_c(w):
-            c.start()
-
-    def finish(w):
-        for c in copies_c(w):
-            c.wait_recv()
+        lax.fori_loop(c * hb, c * hb + quarter, one, 0)
+        for copy in copies_c(w, c):
+            copy.start()
+
+    def finish(w, c):
+        for copy in copies_c(w, c):
+            copy.wait_recv()
 
         def one(b, carry):
+            h = b + quarter
             outs[w][b] = f32(rbs[w][y, b]) + f32(rcs[w][b])
-            outs[w][b + half] = f32(rbs[w][x, b + half]) + f32(rcs[w][b + half])
+            outs[w][h] = f32(rbs[w][x, h]) + f32(rcs[w][h])
             return carry
-        lax.fori_loop(0, half, one, 0)
+        lax.fori_loop(c * hb, c * hb + quarter, one, 0)
 
     make_smat(0)
 
@@ -313,18 +323,17 @@
         sort_out(0, b, mm(inp[:, blk(b)], w1[b], NN).astype(bf))
     each(first)
     pl.semaphore_wait(barrier, ranks - 1 + 3)
-    send_sorted(0)
+    sbuf[0] = stage[...].astype(bf)
+    send(0, 0)
 
     make_pmat(1)
 
     def back_fourth(b):
         unplace(1, 1, b, mm(cot[:, blk(b)], w4[b], NT).astype(bf))
     each(back_fourth)
-    send(1)
+    send(1, 0)
     make_pmat(0)
     make_smat(1)
-
-    arrive(0)
 
     def middle(b):
         m = placed(0, 0, b)
@@ -335,18 +344,19 @@
         h = (0.5 * v * (1.0 + jnp.tanh(GELU_C * (v + GELU_A * (v * v * v))))).astype(bf)
         hid[b] = h
         sort_out(1, b, mm(h, w3[b], NN).astype(bf))
-    each(middle)
-    send_sorted(2)
-
-    arrive(1)
-    stage[...] = f32(rbuf[1])
+    def load(e, c):
+        rows, cut = piece(e, c)
+        stage[:, rows, cut] = f32(rbuf[e, :, rows, cut])
+
+    def forward(c):
+        each(middle, c)
+        rows, cut = piece(2, c)
+        sbuf[2, :, rows, cut] = stage[:, rows, cut].astype(bf)
 
     def third(b):
         t = unsorted(1, b)
         bth[b] = t
         put_grad(2, b, hid[b], t)
-    each(third)
-    copy_a(2).start()
 
     def back_second(b):
         v = f32(pre[b])
@@ -356,49 +366,93 @@
         p = (mm(bth[b], w3[b], NT) * slope).astype(bf)
         bpr[b] = p
         unplace(3, 0, b, mm(p, w2[b], NT).astype(bf))
-    each(back_second)
-    send(3)
-
-    a_to_b(2)
-
     def second(b):
         put_grad(1, b, mup[b], bpr[b])
-    each(second)
-    copy_a(1).start()
-
-    arrive(2)
 
     def fourth(b):
         m = placed(2, 1, b)
         out[:, blk(b)] = mm(m, w4[b], NN).astype(bf)
         put_grad(3, b, m, cot[:, blk(b)])
-    each(fourth)
-    copy_a(3).start()
-    a_to_b(1)
-    a_to_b(3)
-
-    arrive(3)
-    stage[...] = f32(rbuf[3])
-
     def last(b):
         t = unsorted(0, b)
         put_grad(0, b, inp[:, blk(b)], t)
         gin[:, blk(b)] = mm(t, w1[b], NT).astype(bf)
-    each(last)
-    copy_a(0).start()
-    a_to_b(0)
-    for w in (2, 1, 3, 0):
-        b_to_c(w)
-    for w in (2, 1, 3, 0):
-        finish(w)
-
-    for e in range(4):
-        for k in range(1, ranks):
-            hop(e, k).wait_send()
-    for w in range(4):
-        copy_a(w).wait_send()
-        for c in copies_b(w) + copies_c(w):
-            c.wait_send()
+
+    arrive(0, 0)
+    send(0, 1)
+    forward(0)
+    arrive(1, 0)
+    send(1, 1)
+    load(1, 0)
+    each(third, 0)
+    copy_a(2, 0).start()
+    each(back_second, 0)
+    a_to_b(2, 0)
+    each(second, 0)
+    copy_a(1, 0).start()
+
+    arrive(0, 1)
+    send(2, 0)
+    forward(1)
+    a_to_b(1, 0)
+    arrive(1, 1)
+    send(2, 1)
+    send(3, 0)
+    load(1, 1)
+    each(third, 1)
+    copy_a(2, 1).start()
+    each(back_second, 1)
+    send(3, 1)
+    a_to_b(2, 1)
+    each(second, 1)
+    copy_a(1, 1).start()
+    b_to_c(2, 0)
+    a_to_b(1, 1)
+    b_to_c(1, 0)
+
+    for c in range(2):
+        arrive(2, c)
+    for c in range(2):
+        each(fourth, c)
+        copy_a(3, c).start()
+    for c in range(2):
+        a_to_b(3, c)
+    b_to_c(2, 1)
+
+    for c in range(2):
+        arrive(3, c)
+    stage[...] = f32(rbuf[3])
+    for c in range(2):
+        each(last, c)
+        copy_a(0, c).start()
+    for c in range(2):
+        a_to_b(0, c)
+    order = [(1, 1), (3, 0), (3, 1), (0, 0), (0, 1)]
+    for w, c in order:
+        b_to_c(w, c)
+    for w, c in [(2, 0), (1, 0), (2, 1)] + order:
+        finish(w, c)
+
+    for c in range(2):
+        for e in range(4):
+            for k in range(1, ranks):
+                hop(e, c, k).wait_send()
+        for w in range(4):
+            copy_a(w, c).wait_send()
+            for copy in copies_b(w, c) + copies_c(w, c):
+                copy.wait_send()
+
+
+def hand_on(*refs):
+    n = len(refs) // 2
+    sem = refs[-1]
+    copies = [
+        pltpu.make_async_copy(refs[i], refs[n + i], sem.at[i]) for i in range(n)
+    ]
+    for copy in copies:
+        copy.start()
+    for copy in copies:
+        copy.wait()
 
 
 def fused_body(inputs, cotangent, w_first, w_second, w_third, w_fourth, route_up, route_down):
@@ -429,12 +483,12 @@
     scratch += [vm((2, nblk) + s, bf) for s in shapes]
     scratch += [vm((nblk,) + s, bf) for s in shapes]
     dma = pltpu.SemaphoreType.DMA
-    scratch += [dma((4, ranks - 1)), dma((4, ranks - 1)), dma((4,)), dma((4,))]
-    scratch += [dma((4, 2))] * 4
+    scratch += [dma((4, 2, ranks - 1))] * 2 + [dma((4, 2))] * 2
+    scratch += [dma((4, 2, 2))] * 4
     out_shape = [jax.ShapeDtypeStruct((tok, width), bf)] * 2
     out_shape += [jax.ShapeDtypeStruct((nblk,) + s, jnp.float32) for s in shapes]
     spec = pl.BlockSpec(memory_space=pltpu.VMEM)
-    return tuple(pl.pallas_call(
+    results = pl.pallas_call(
         functools.partial(layer_kernel, ranks, nblk, tok, bw, hw, scale),
         out_shape=out_shape,
         in_specs=[spec] * 8,
@@ -442,7 +496,15 @@
         scratch_shapes=scratch,
         compiler_params=pltpu.CompilerParams(
             collective_id=0, has_side_effects=True, vmem_limit_bytes=60 * 1024 * 1024),
-    )(inputs, cotangent, *weights, slot, cols))
+    )(inputs, cotangent, *weights, slot, cols)
+    anywhere = pl.BlockSpec(memory_space=pl.ANY)
+    return tuple(pl.pallas_call(
+        hand_on,
+        out_shape=out_shape,
+        in_specs=[anywhere] * 6,
+        out_specs=[anywhere] * 6,
+        scratch_shapes=[dma((6,))],
+    )(*results))
 
 
 def solution(mesh):
@@ -451,7 +513,7 @@
         ranks, dps = mesh.shape["tensor"], mesh.shape["dp"]
         nblk, bw = w_first.shape[:2]
         aligned = (
-            dps == 8 and nblk % 2 == 0 and bw // (nblk * ranks) == 8
+            dps == 8 and nblk % 4 == 0 and bw // (nblk * ranks) == 8
             and (bw // dps) % 16 == 0 and (w_third.shape[1] // dps) % 16 == 0
             and (bw // ranks) % 16 == 0 and inputs.shape[0] % 128 == 0
         )

time: 106 us -> 187 us (1.76)
  Pallas kernels: 90.5 us -> 181 us
  local copies, waits for them, and re-layouts: 12.4 us -> 3.09 us
    pallas_call x0 -> x1, Pallas kernels: none -> 104 us  [fused_body(): pl.pallas_call(hand_on, out_shape=out_shape, in_specs=[anywhere] * 6, out...]
    pallas_call x1, Pallas kernels: 90.5 us -> 77 us  [fused_body(): pl.pallas_call(functools.partial(layer_kernel, ranks, nblk, tok, bw, hw,...]
    unnamed x11 -> x1, local copies, waits for them, and re-layouts: 9.33 us -> 0.01 us
where the time goes in v1:
time: 187 us
  Pallas kernels  181 us (97%)
  local copies, waits for them, and re-layouts  3.09 us (2%)
    pallas_call x1, Pallas kernels, fused_body(): pl.pallas_call(hand_on, out_shape=out_shape, in_specs=[anywhere] * 6, out...  104 us
    pallas_call x1, Pallas kernels, fused_body(): pl.pallas_call(functools.partial(layer_kernel, ranks, nblk, tok, bw, hw,...  77 us

profile of v1, /device:TPU:8, one launch (start us, length us, event | category | flops | bytes accessed | tf_op | source)
XLA Modules:
  0.0 187.2 jit_solution(15834100307389311799)
XLA Ops:
  0.6 0.8 stack.9
  1.4 0.8 stack.10
  2.3 0.7 select_reduce_fusion.1
  3.0 0.1 broadcast_subtract_fusion
  3.0 1.2 select_reduce_fusion
  4.2 0.6 constant_dynamic-slice_fusion.slot
  4.8 0.1 copy.15
  4.9 0.8 copy.16
  5.8 77.0 %shard_map.127 = (bf16[128,2048]{1,0:T(8,128)(2,1)}, bf16[128,2048]{1,0:T(8,128)(2,1)}, f32[8,32,256]{2,1,0:T(8,128)}, f32[8,32,896]{2,1,0:T(8,128)}, f32[8,112,256]{2,1,0:T(8,128)}, /*index=5*/f32[8,32,256]{2,1,0:T(8,128)}) custom-call(bf16[128,2048]{1,0:T(8,128)(2,1)} %inp.1, bf16[128,2048]{1,0:T(8,128)(2,1)} %cot.1, bf16[8,256,256]{2,1,0:T(8,128)(2,1)} %w1.1, ...), custom_call_target="tpu_custom_call" | custom-call | tf_op jit(solution)/shard_map/pallas_call | solution.py:491
  82.8 104.4 %shard_map.128 = (bf16[128,2048]{1,0:T(8,128)(2,1)}, bf16[128,2048]{1,0:T(8,128)(2,1)}, f32[8,32,256]{2,1,0:T(8,128)}, f32[8,32,896]{2,1,0:T(8,128)}, f32[8,112,256]{2,1,0:T(8,128)}, /*index=5*/f32[8,32,256]{2,1,0:T(8,128)}) custom-call(bf16[128,2048]{1,0:T(8,128)(2,1)} %get-tuple-element.12.refs_0_, bf16[128,2048]{1,0:T(8,128)(2,1)} %get-tuple-element.13.refs_1_, ...), custom_call_target="tpu_custom_call" | custom-call | tf_op jit(solution)/shard_map/pallas_call | solution.py:501
  (3 shorter events, 0.0 us)

commit v2 on v1

--- a/solution.py
+++ b/solution.py
@@ -444,15 +444,18 @@
 
 
 def hand_on(*refs):
-    n = len(refs) // 2
-    sem = refs[-1]
-    copies = [
-        pltpu.make_async_copy(refs[i], refs[n + i], sem.at[i]) for i in range(n)
-    ]
-    for copy in copies:
-        copy.start()
-    for copy in copies:
-        copy.wait()
+    n = (len(refs) - 2) // 3
+    arrived, left = refs[3 * n:]
+    held = refs[2 * n:3 * n]
+    loads = [pltpu.make_async_copy(refs[i], held[i], arrived.at[i]) for i in range(n)]
+    stores = [pltpu.make_async_copy(held[i], refs[n + i], left.at[i]) for i in range(n)]
+    for load in loads:
+        load.start()
+    for load, store in zip(loads, stores):
+        load.wait()
+        store.start()
+    for store in stores:
+        store.wait()
 
 
 def fused_body(inputs, cotangent, w_first, w_second, w_third, w_fourth, route_up, route_down):
@@ -503,7 +506,8 @@
         out_shape=out_shape,
         in_specs=[anywhere] * 6,
         out_specs=[anywhere] * 6,
-        scratch_shapes=[dma((6,))],
+        scratch_shapes=[vm(o.shape, o.dtype) for o in out_shape] + [dma((6,)), dma((6,))],
+        compiler_params=pltpu.CompilerParams(vmem_limit_bytes=32 * 1024 * 1024),
     )(*results))
 
 

time: 187 us -> 92 us (0.49)
  Pallas kernels: 181 us -> 79.4 us
  local copies, waits for them, and re-layouts: 3.09 us -> 9.42 us
    pallas_call x1, Pallas kernels: 104 us -> 2.39 us  [fused_body(): pl.pallas_call(hand_on, out_shape=out_shape, in_specs=[anywhere] * 6, out...]
    unnamed x1 -> x13, local copies, waits for them, and re-layouts: 0.01 us -> 6.34 us
where the time goes in v2:
time: 92 us; the launch traced here: 91.5 us
  Pallas kernels  79.4 us (86%)
  local copies, waits for them, and re-layouts  9.42 us (10%)
  other arithmetic  1.26 us (1%)
    pallas_call x1, Pallas kernels, fused_body(): pl.pallas_call(functools.partial(layer_kernel, ranks, nblk, tok, bw, hw,...  77 us
    unnamed x13, local copies, waits for them, and re-layouts  6.34 us
    pallas_call x1, Pallas kernels, fused_body(): pl.pallas_call(hand_on, out_shape=out_shape, in_specs=[anywhere] * 6, out...  2.39 us

profile of v2, /device:TPU:8, one launch (start us, length us, event | category | flops | bytes accessed | tf_op | source)
XLA Modules:
  0.0 91.5 jit_solution(2291827348138960804)
XLA Ops:
  0.6 0.8 stack.9
  1.4 0.8 stack.10
  2.3 0.7 select_reduce_fusion.1
  3.0 0.1 broadcast_subtract_fusion
  3.0 1.2 %select_reduce_fusion = s32[2,32,64]{2,1,0:T(8,128)S(1)} fusion(s32[2,32,256]{2,1,0:T(8,128)S(1)} %get-tuple-element.20, s32[2,32,256]{2,1,0:T(8,128)S(1)} %get-tuple-element.18), kind=kLoop, calls=%fused_computation | loop fusion | flops 3141632 | bytes 147456 | tf_op jit(solution)/shard_map/reduce_sum | solution.py:158
  4.2 0.6 constant_dynamic-slice_fusion.slot
  4.8 0.1 copy.15
  4.9 0.8 copy.16
  5.8 77.0 %shard_map.127 = (bf16[128,2048]{1,0:T(8,128)(2,1)}, bf16[128,2048]{1,0:T(8,128)(2,1)}, f32[8,32,256]{2,1,0:T(8,128)}, f32[8,32,896]{2,1,0:T(8,128)}, f32[8,112,256]{2,1,0:T(8,128)}, /*index=5*/f32[8,32,256]{2,1,0:T(8,128)}) custom-call(bf16[128,2048]{1,0:T(8,128)(2,1)} %inp.1, bf16[128,2048]{1,0:T(8,128)(2,1)} %cot.1, bf16[8,256,256]{2,1,0:T(8,128)(2,1)} %w1.1, ...), custom_call_target="tpu_custom_call" | custom-call | tf_op jit(solution)/shard_map/pallas_call | solution.py:494
  82.8 0.0 copy-start
  82.8 1.2 %copy-done = f32[8,32,896]{2,1,0:T(8,128)S(1)} copy-done((f32[8,32,896]{2,1,0:T(8,128)S(1)}, f32[8,32,896]{2,1,0:T(8,128)}, u32[]{:S(2)}) %copy-start) | copy-done | bytes 917528
  84.0 0.0 copy-start.1
  84.0 1.2 %copy-done.1 = f32[8,112,256]{2,1,0:T(8,128)S(1)} copy-done((f32[8,112,256]{2,1,0:T(8,128)S(1)}, f32[8,112,256]{2,1,0:T(8,128)}, u32[]{:S(2)}) %copy-start.1) | copy-done | bytes 917528
  85.1 0.0 copy-start.2
  85.1 1.0 %copy-done.2 = bf16[128,2048]{1,0:T(8,128)(2,1)S(1)} copy-done((bf16[128,2048]{1,0:T(8,128)(2,1)S(1)}, bf16[128,2048]{1,0:T(8,128)(2,1)}, u32[]{:S(2)}) %copy-start.2) | copy-done | bytes 524312
  86.2 0.0 copy-start.3
  86.2 1.0 %copy-done.3 = bf16[128,2048]{1,0:T(8,128)(2,1)S(1)} copy-done((bf16[128,2048]{1,0:T(8,128)(2,1)S(1)}, bf16[128,2048]{1,0:T(8,128)(2,1)}, u32[]{:S(2)}) %copy-start.3) | copy-done | bytes 524312
  87.2 0.0 copy-start.4
  87.2 0.9 %copy-done.4 = f32[8,32,256]{2,1,0:T(8,128)S(1)} copy-done((f32[8,32,256]{2,1,0:T(8,128)S(1)}, f32[8,32,256]{2,1,0:T(8,128)}, u32[]{:S(2)}) %copy-start.4) | copy-done | bytes 262168
  88.2 0.0 copy-start.5
  88.2 0.9 %copy-done.5 = f32[8,32,256]{2,1,0:T(8,128)S(1)} copy-done((f32[8,32,256]{2,1,0:T(8,128)S(1)}, f32[8,32,256]{2,1,0:T(8,128)}, u32[]{:S(2)}) %copy-start.5) | copy-done | bytes 262168
  89.1 2.4 %shard_map.128 = (bf16[128,2048]{1,0:T(8,128)(2,1)}, bf16[128,2048]{1,0:T(8,128)(2,1)}, f32[8,32,256]{2,1,0:T(8,128)}, f32[8,32,896]{2,1,0:T(8,128)}, f32[8,112,256]{2,1,0:T(8,128)}, /*index=5*/f32[8,32,256]{2,1,0:T(8,128)}) custom-call(bf16[128,2048]{1,0:T(8,128)(2,1)S(1)} %copy-done.2, bf16[128,2048]{1,0:T(8,128)(2,1)S(1)} %copy-done.3, ...), custom_call_target="tpu_custom_call" | custom-call | tf_op jit(solution)/shard_map/pallas_call | solution.py:504
  (3 shorter events, 0.0 us)
Async XLA Ops:
  82.8 1.2 %copy-start = (f32[8,32,896]{2,1,0:T(8,128)S(1)}, f32[8,32,896]{2,1,0:T(8,128)}, u32[]{:S(2)}) copy-start(f32[8,32,896]{2,1,0:T(8,128)} %get-tuple-element.15.refs_3_) | copy-start | bytes 2752516
  84.0 1.2 %copy-start.1 = (f32[8,112,256]{2,1,0:T(8,128)S(1)}, f32[8,112,256]{2,1,0:T(8,128)}, u32[]{:S(2)}) copy-start(f32[8,112,256]{2,1,0:T(8,128)} %get-tuple-element.16.refs_4_) | copy-start | bytes 2752516
  85.1 1.0 %copy-start.2 = (bf16[128,2048]{1,0:T(8,128)(2,1)S(1)}, bf16[128,2048]{1,0:T(8,128)(2,1)}, u32[]{:S(2)}) copy-start(bf16[128,2048]{1,0:T(8,128)(2,1)} %get-tuple-element.12.refs_0_) | copy-start | bytes 1572868
  86.2 1.0 %copy-start.3 = (bf16[128,2048]{1,0:T(8,128)(2,1)S(1)}, bf16[128,2048]{1,0:T(8,128)(2,1)}, u32[]{:S(2)}) copy-start(bf16[128,2048]{1,0:T(8,128)(2,1)} %get-tuple-element.13.refs_1_) | copy-start | bytes 1572868
  87.2 0.9 %copy-start.4 = (f32[8,32,256]{2,1,0:T(8,128)S(1)}, f32[8,32,256]{2,1,0:T(8,128)}, u32[]{:S(2)}) copy-start(f32[8,32,256]{2,1,0:T(8,128)} %get-tuple-element.14.refs_2_) | copy-start | bytes 786436
  88.2 0.9 %copy-start.5 = (f32[8,32,256]{2,1,0:T(8,128)S(1)}, f32[8,32,256]{2,1,0:T(8,128)}, u32[]{:S(2)}) copy-start(f32[8,32,256]{2,1,0:T(8,128)} %get-tuple-element.17.refs_5_) | copy-start | bytes 786436
